TPU v7x, 512 devices: a whole 4x4x16 slice. The times are simulated.
512 devices in a mesh: group: 16 (over x, y_lo, core), head: 32 (over z, y_hi).
Axes of the slice: x: 4, y: 4 (y_hi: 2, y_lo: 2; y = y_hi * 2 + y_lo), z: 16, core: 2. Of those that a mesh axis runs over, the one named last changes fastest.
Arguments:
- enc_resid: bfloat16 [1024, 1024], P('group'), may hold values from -6 to 6
- enc_qkv: bfloat16 [3, 1024, 16384], P(None, 'group', 'head'), may hold values from -6 to 6
- enc_bias: float32 [64, 64], replicated, may hold values from -4 to 315
- out_weight: bfloat16 [16384, 1024], P(('head', 'group')), may hold values from -0.046875 to 0.046875
- final_gain: float32 [1024], replicated, may hold values from 0.25 to 1.75
- key_weight: bfloat16 [1024, 16384], P('group', 'head'), may hold values from -0.1875 to 0.1875
- value_weight: bfloat16 [1024, 16384], P('group', 'head'), may hold values from -0.1875 to 0.1875
- dec_query: bfloat16 [6144, 16384], P('group', 'head'), may hold values from -6 to 6
- cross_bias: float32 [384, 64], replicated, may hold values from -4 to 315
- out_grad: bfloat16 [6144, 16384], P('group', 'head'), may hold values from -6 to 6
- sources: int32 [16, 3], replicated, may hold values from 0 to 15, all different within a row
- head_keep: int32 [16, 128], P('group', 'head'), may hold values 0 or 1
Outputs:
- context: bfloat16 [6144, 16384], P('group', 'head')
- memory_grad: bfloat16 [1024, 1024], P('group')
Inputs may be any that keep to these rules, and one draw needn't show every extreme that they name: `sources`: each row names 3 different encoder groups; every encoder group is named by some row.
All inputs are finite; a program needn't handle non-finite values. No bound on the sum of `head_keep` on one device may be relied on, other than what follows from the above.
Results may differ from a plain program's by a relative error of at most 0.034.
Values may be sent and summed in bfloat16 or wider, within the bound.
A program may use at most 64 MiB of HBM per device.

v0:
```python
import math

import jax
import jax.numpy as jnp
from jax import lax
from jax.sharding import PartitionSpec as P

DK = 128
SEQ = 64
QROWS = 384
MEM = 3


def softmax_rows(scores):
    top = jnp.max(scores, axis=-1, keepdims=True)
    expd = jnp.exp(scores - top)
    return expd / jnp.sum(expd, axis=-1, keepdims=True)


def norm_rows(memory, gain):
    inv = lax.rsqrt(jnp.mean(memory * memory, axis=-1, keepdims=True) + 1e-06)
    return (memory * inv * gain).astype(jnp.bfloat16)


def norm_grad(memory, upstream, gain):
    inv = lax.rsqrt(jnp.mean(memory * memory, axis=-1, keepdims=True) + 1e-06)
    normed = memory * inv
    scaled = upstream * gain
    return (inv * (scaled - normed * jnp.mean(scaled * normed, axis=-1, keepdims=True))).astype(
        jnp.bfloat16
    )


def times_transposed(left, weight):
    return lax.dot_general(
        left, weight, (((1,), (1,)), ((), ())), preferred_element_type=jnp.float32
    )


def shards(
    enc_resid,
    enc_qkv,
    enc_bias,
    out_weight,
    final_gain,
    key_weight,
    value_weight,
    dec_query,
    cross_bias,
    out_grad,
    sources,
    head_keep,
):
    scale = 1.0 / math.sqrt(DK)
    width = enc_qkv.shape[2]
    nheads = width // DK
    mine = lax.axis_index("group")
    enc_q = enc_qkv[0].reshape(SEQ, nheads, DK)
    enc_k = enc_qkv[1].reshape(SEQ, nheads, DK)
    enc_v = enc_qkv[2].reshape(SEQ, nheads, DK)
    enc_scores = (
        jnp.einsum("qhd,khd->hqk", enc_q, enc_k, preferred_element_type=jnp.float32) * scale
        + enc_bias
    )
    enc_prob = softmax_rows(enc_scores).astype(jnp.bfloat16)
    enc_ctx = jnp.einsum("hqk,khd->qhd", enc_prob, enc_v, preferred_element_type=jnp.float32)
    enc_ctx = enc_ctx.astype(jnp.bfloat16).reshape(SEQ, width)
    partial_out = jnp.dot(
        enc_ctx,
        lax.all_gather(out_weight, "group", axis=0, tiled=True),
        preferred_element_type=jnp.float32,
    )
    key_full, value_full = (
        lax.all_gather(key_weight, "group", axis=0, tiled=True),
        lax.all_gather(value_weight, "group", axis=0, tiled=True),
    )
    memory = enc_resid.astype(jnp.float32) + lax.psum(partial_out, "head")
    mem_norm = norm_rows(memory, final_gain)
    keys = jnp.dot(mem_norm, key_full, preferred_element_type=jnp.float32).astype(jnp.bfloat16)
    values = jnp.dot(mem_norm, value_full, preferred_element_type=jnp.float32).astype(jnp.bfloat16)
    paired = jnp.concatenate([keys, values], axis=1)
    my_sources = lax.dynamic_index_in_dim(sources, mine, 0, keepdims=False)
    every_pair = lax.all_gather(paired, "group", axis=0, tiled=True)
    chosen = jnp.concatenate(
        [
            lax.dynamic_slice_in_dim(every_pair, my_sources[slot] * SEQ, SEQ, 0)
            for slot in range(MEM)
        ],
        axis=0,
    )
    mem_keys = chosen[:, :width].reshape(MEM * SEQ, nheads, DK)
    mem_values = chosen[:, width:].reshape(MEM * SEQ, nheads, DK)
    query = dec_query.reshape(QROWS, nheads, DK)
    keep_low = head_keep[0].astype(jnp.bfloat16)
    bias_all = jnp.tile(cross_bias, (1, MEM))
    cross = (
        jnp.einsum("qhd,khd->hqk", query, mem_keys, preferred_element_type=jnp.float32) * scale
        + bias_all
    )
    prob = softmax_rows(cross)
    prob_low = prob.astype(jnp.bfloat16)
    attn = jnp.einsum("hqk,khd->qhd", prob_low, mem_values, preferred_element_type=jnp.float32)
    context = (
        (attn * keep_low.astype(jnp.float32)[None, :, None])
        .astype(jnp.bfloat16)
        .reshape(QROWS, width)
    )
    grad = out_grad.reshape(QROWS, nheads, DK) * keep_low[None, :, None]
    dprob = jnp.einsum("qhd,khd->hqk", grad, mem_values, preferred_element_type=jnp.float32)
    delta = jnp.sum(prob * dprob, axis=-1, keepdims=True)
    dscore = (prob * (dprob - delta) * scale).astype(jnp.bfloat16)
    dk_part = jnp.einsum("hqk,qhd->khd", dscore, query, preferred_element_type=jnp.float32).astype(
        jnp.bfloat16
    )
    dv_part = jnp.einsum("hqk,qhd->khd", prob_low, grad, preferred_element_type=jnp.float32).astype(
        jnp.bfloat16
    )
    dpair = jnp.concatenate(
        [dk_part.reshape(MEM, SEQ, width), dv_part.reshape(MEM, SEQ, width)], axis=2
    )
    flat_sources = sources.reshape(-1)
    picked = (flat_sources == mine).astype(jnp.float32)
    summed = jnp.einsum(
        "m,mrc->rc", picked, lax.all_gather(dpair, "group", axis=0, tiled=True).astype(jnp.float32)
    )
    summed = summed.astype(jnp.bfloat16)
    dnorm_part = times_transposed(summed[:, :width], key_full) + times_transposed(
        summed[:, width:], value_full
    )
    dnorm = lax.psum(dnorm_part.astype(jnp.bfloat16), "head").astype(jnp.float32)
    memory_grad = norm_grad(memory, dnorm, final_gain)
    return (context, memory_grad)


def solution(mesh):
    in_specs = (
        P("group", None),
        P(None, "group", "head"),
        P(),
        P(("head", "group"), None),
        P(),
        P("group", "head"),
        P("group", "head"),
        P("group", "head"),
        P(),
        P("group", "head"),
        P(),
        P("group", "head"),
    )
    out_specs = (P("group", "head"), P("group", None))
    return jax.shard_map(shards, mesh=mesh, in_specs=in_specs, out_specs=out_specs, check_vma=False)
```

profile of v0, /device:TPU:2, one launch (start us, length us, event | category | flops | bytes accessed | tf_op | source)
XLA Modules:
  0.0 869.8 jit_solution(4122692869663150683)
XLA Ops:
  7.2 0.7 all-gather.6.cloned.1.call-update
  8.0 0.8 copy.42
  8.8 0.9 fusion.64
  10.3 44.2 %all-gather.6.cloned.1.call-done = bf16[512,1024]{1,0:T(8,128)(2,1)} async-done(((bf16[32,1024]{1,0:T(8,128)(2,1)}), bf16[512,1024]{1,0:T(8,128)(2,1)}) %all-gather.6.cloned.1.call-update) | async-done | bytes 1048592 | tf_op jit(solution)/shard_map/all_gather | solution.py:70
  54.4 2.2 fusion.41
  56.7 0.7 all-gather.10.cloned.1.call-update
  57.5 0.5 all-gather.8.cloned.1.call-update
  58.0 306.3 %all-reduce.3.cloned.1.call-done = f32[64,1024]{1,0:T(8,128)} async-done(((f32[64,1024]{1,0:T(8,128)}), f32[64,1024]{1,0:T(8,128)}) %all-reduce.3.cloned.1.call-update) | async-done | bytes 262160 | tf_op jit(solution)/shard_map/psum | solution.py:77
  364.3 1.1 multiply_reduce_fusion.2
  365.4 1.0 multiply_convert_fusion.1
  366.5 35.7 %all-gather.10.cloned.1.call-done = bf16[1024,512]{1,0:T(8,128)(2,1)} async-done(((bf16[64,512]{1,0:T(8,128)(2,1)}), bf16[1024,512]{1,0:T(8,128)(2,1)}) %all-gather.10.cloned.1.call-update) | async-done | bytes 1048592 | tf_op jit(solution)/shard_map/all_gather | solution.py:75
  402.2 1.5 convolution_convert_fusion.1
  403.8 41.0 %all-gather.8.cloned.1.call-done = bf16[1024,512]{1,0:T(8,128)(2,1)} async-done(((bf16[64,512]{1,0:T(8,128)(2,1)}), bf16[1024,512]{1,0:T(8,128)(2,1)}) %all-gather.8.cloned.1.call-update) | async-done | bytes 1048592 | tf_op jit(solution)/shard_map/all_gather | solution.py:74
  444.7 1.5 convolution_convert_fusion.2
  446.2 0.7 pad_maximum_fusion.2
  447.1 0.6 fusion.65
  449.7 39.5 %all-gather.12.cloned.1.call-done = bf16[1024,1024]{1,0:T(8,128)(2,1)} async-done(((bf16[64,1024]{1,0:T(8,128)(2,1)}), bf16[1024,1024]{1,0:T(8,128)(2,1)}) %all-gather.12.cloned.1.call-update) | async-done | bytes 2097168 | tf_op jit(solution)/shard_map/all_gather | solution.py:83
  489.2 1.1 constant_dynamic-slice_fusion.2
  490.4 0.5 fusion.67
  490.9 0.5 copy-done.5
  492.6 2.2 fusion.19
  495.0 0.8 pad_maximum_fusion.1
  496.3 50.1 %all-gather.14.cloned.1.call-done = bf16[48,64,1024]{2,1,0:T(8,128)(2,1)} async-done(((bf16[3,64,1024]{2,1,0:T(8,128)(2,1)}), bf16[48,64,1024]{2,1,0:T(8,128)(2,1)}) %all-gather.14.cloned.1.call-update) | async-done | bytes 6291472 | tf_op jit(solution)/shard_map/all_gather | solution.py:124
  546.4 9.5 %fusion.3 = bf16[1,64,1024]{2,0,1:T(2,128)(2,1)S(1)} fusion(pred[48,1,1]{0,1,2:T(4,128)(4,1)S(1)} %reshape.86, bf16[48,64,1024]{2,1,0:T(8,128)(2,1)} %all-gather.14.cloned.1.call-done), kind=kOutput, calls=%fused_computation.3 | convolution fusion | flops 6291456 | bytes 6422576 | tf_op jit(solution)/shard_map/m,mrc->rc/dot_general | solution.py:123
  556.0 0.4 fusion.45
  556.4 0.7 copy-done.2
  557.2 1.1 fusion.18
  558.3 1.7 fusion.14
  560.0 0.9 copy.55
  560.9 299.3 %all-reduce.5.cloned.1.call-done = bf16[64,1024]{1,0:T(8,128)(2,1)} async-done(((bf16[64,1024]{1,0:T(8,128)(2,1)}), bf16[64,1024]{1,0:T(8,128)(2,1)}) %all-reduce.5.cloned.1.call-update) | async-done | bytes 131088 | tf_op jit(solution)/shard_map/psum | solution.py:130
  860.2 1.1 multiply_reduce_fusion.1
  861.3 1.7 multiply_convert_fusion
  (54 shorter events, 2.9 us)
Async XLA Ops:
  7.2 483.2 %copy-start = (bf16[384,512]{1,0:T(8,128)(2,1)S(1)}, bf16[384,512]{1,0:T(8,128)(2,1)}, u32[]{:S(2)}) copy-start(bf16[384,512]{1,0:T(8,128)(2,1)} %param.19) | copy-start | bytes 1179652
  7.2 47.3 %all-gather.6.cloned.1.call-start = ((), (), s32[]{:S(2)}) async-start(), calls=%async_computation | async-start | bytes 1114112 | tf_op jit(solution)/shard_map/all_gather | solution.py:70
  7.9 356.4 %all-reduce.3.cloned.1.call-start = ((), (), s32[]{:S(2)}) async-start(), calls=%async_computation.1 | async-start | bytes 524288 | tf_op jit(solution)/shard_map/psum | solution.py:77
  10.0 354.3 %copy-start.4 = (bf16[64,1024]{1,0:T(8,128)(2,1)S(1)}, bf16[64,1024]{1,0:T(8,128)(2,1)}, u32[]{:S(2)}) copy-start(bf16[64,1024]{1,0:T(8,128)(2,1)} %param.12) | copy-start | bytes 393220
  10.3 355.2 %copy-start.7 = (f32[1024]{0:T(1024)S(1)}, f32[1024]{0:T(1024)}, u32[]{:S(2)}) copy-start(f32[1024]{0:T(1024)} %param.16) | copy-start | bytes 12292
  56.7 345.6 %all-gather.10.cloned.1.call-start = ((), (), s32[]{:S(2)}) async-start(), calls=%async_computation.3 | async-start | bytes 1114112 | tf_op jit(solution)/shard_map/all_gather | solution.py:75
  57.4 387.3 %all-gather.8.cloned.1.call-start = ((), (), s32[]{:S(2)}) async-start(), calls=%async_computation.2 | async-start | bytes 1114112 | tf_op jit(solution)/shard_map/all_gather | solution.py:74
  58.0 431.2 %all-gather.12.cloned.1.call-start = ((), (), s32[]{:S(2)}) async-start(), calls=%async_computation.4 | async-start | bytes 2228224 | tf_op jit(solution)/shard_map/all_gather | solution.py:83
  366.5 80.5 %copy-start.8 = (s32[16,3]{0,1:T(4,128)S(1)}, s32[16,3]{0,1:T(4,128)}, u32[]{:S(2)}) copy-start(s32[16,3]{0,1:T(4,128)} %param.22) | copy-start | bytes 580
  366.5 83.1 %copy-start.9 = (s32[1,4]{1,0:T(1,128)S(1)}, s32[1,4]{1,0:T(1,128)}, u32[]{:S(2)}) copy-start(s32[1,4]{1,0:T(1,128)} %param.23) | copy-start | bytes 52
  446.9 99.4 %all-gather.14.cloned.1.call-start = ((), (), s32[]{:S(2)}) async-start(), calls=%async_computation.5 | async-start | bytes 6684672 | tf_op jit(solution)/shard_map/all_gather | solution.py:124
  449.7 40.7 %copy-start.6 = (f32[384,64]{0,1:T(8,128)S(1)}, f32[384,64]{0,1:T(8,128)}, u32[]{:S(2)}) copy-start(f32[384,64]{0,1:T(8,128)} %param.20) | copy-start | bytes 294916
  490.4 1.0 copy-start.5
  490.9 1.0 copy-start.10
  495.8 364.3 %all-reduce.5.cloned.1.call-start = ((), (), s32[]{:S(2)}) async-start(), calls=%async_computation.6 | async-start | bytes 262144 | tf_op jit(solution)/shard_map/psum | solution.py:130
  496.3 59.7 %copy-start.3 = (bf16[1024,512]{1,0:T(8,128)(2,1)S(1)}, bf16[1024,512]{1,0:T(8,128)(2,1)}, u32[]{:S(2)}) copy-start(bf16[1024,512]{1,0:T(8,128)(2,1)} %all-gather.8.cloned.1.call-done) | copy-start | bytes 3145732
  555.9 1.2 copy-start.2
  558.3 301.9 %copy-start.1 = (f32[64,1024]{1,0:T(8,128)S(1)}, f32[64,1024]{1,0:T(8,128)}, u32[]{:S(2)}) copy-start(f32[64,1024]{1,0:T(8,128)} %all-reduce.3.cloned.1.call-done) | copy-start | bytes 786436
Sparse Core Ops, SparseCore 0:
  10.2 44.2 all-gather.5
  57.9 306.3 all-reduce.2
  366.7 35.4 all-gather.9
  404.5 40.2 all-gather.7
  447.5 41.6 all-gather.11
  495.9 50.3 all-gather.13
  558.4 301.7 all-reduce.4
where the time goes:
time: 870 us
  waiting for transfers between devices  818 us (94%)
  matrix products  21.8 us (3%)
  between operations  16.4 us (2%)
    psum x1, waiting for transfers between devices, shards(): memory = enc_resid.astype(jnp.float32) + lax.psum(partial_out, 'head')  306 us
    psum x1, waiting for transfers between devices, shards(): lax.psum(dnorm_part.astype(jnp.bfloat16), 'head').astype(jnp.float32)  299 us
    all_gather x1, waiting for transfers between devices, shards(): lax.all_gather(dpair, 'group', axis=0, tiled=True).astype(jnp.float32)  50.1 us
    all_gather x1, waiting for transfers between devices, shards(): lax.all_gather(out_weight, 'group', axis=0, tiled=True)  44.2 us
    all_gather x1, waiting for transfers between devices, shards(): lax.all_gather(key_weight, 'group', axis=0, tiled=True)  41 us
    all_gather x1, waiting for transfers between devices, shards(): every_pair = lax.all_gather(paired, 'group', axis=0, tiled=True)  39.5 us
    all_gather x1, waiting for transfers between devices, shards(): lax.all_gather(value_weight, 'group', axis=0, tiled=True)  35.7 us
  transfers between devices with their start and end apart: 7, of which 7 were waited for; matrix products, arithmetic and copies ran while one was open for 1% of the time, Pallas kernels for 0%

commit v1 on v0

v1 whole, which is shorter than its diff:
```python
import functools
import math

import jax
import jax.numpy as jnp
from jax import lax
from jax.experimental import pallas as pl
from jax.experimental.pallas import tpu as pltpu
from jax.sharding import PartitionSpec as P

MESH = pl.DeviceIdType.MESH
BF16 = jnp.bfloat16
F32 = jnp.float32
DK = 128
LANES = 128
EPS = 1e-06


def mm(a, b, ca, cb):
    return lax.dot_general(a, b, (((ca,), (cb,)), ((), ())), preferred_element_type=F32)


def kernel(
    ngroup,
    nhead,
    mem,
    sources,
    keep,
    resid,
    qkv,
    enc_bias,
    gain,
    cross_bias,
    out_w,
    key_w,
    value_w,
    query_hbm,
    grad_hbm,
    context_hbm,
    memory_grad,
    wo,
    kw,
    vw,
    query,
    grad,
    context,
    flat,
    resid_flat,
    out_send,
    out_recv,
    norm_all,
    norm_pick,
    dn_send,
    dn_recv,
    dn_all,
    mg_all,
    local_sem,
    context_sem,
    wo_send,
    wo_recv,
    wo_pass_send,
    wo_pass_recv,
    kv_send,
    kv_recv,
    kv_pass_send,
    kv_pass_recv,
    phase_send,
    phase_recv,
):
    seq, dim = resid.shape
    width = query.shape[1]
    nheads = width // DK
    chunks = dim // LANES
    own_rows = seq // nhead
    blk = own_rows * chunks
    scale = 1.0 / math.sqrt(DK)
    g = lax.axis_index("group")
    h = lax.axis_index("head")
    core = lax.rem(g, 2)
    chip = lax.div(g, 2)
    sibling = g + 1 - 2 * core
    nchip = ngroup // 2

    def each(n, body):
        lax.fori_loop(1, n, lambda k, c: (body(k), c)[1], 0)

    def group_peer(k):
        return lax.rem(g + k, ngroup)

    def head_peer(k):
        return lax.rem(h + k, nhead)

    def remote(src, dst, send, recv, where):
        return pltpu.make_async_remote_copy(
            src_ref=src,
            dst_ref=dst,
            send_sem=send,
            recv_sem=recv,
            device_id=where,
            device_id_type=MESH,
        )

    def total(ref, send, recv):
        return remote(ref, ref, send, recv, {"group": sibling})

    barrier = pltpu.get_barrier_semaphore()
    each(ngroup, lambda k: pl.semaphore_signal(barrier, inc=1, device_id={"group": group_peer(k)}, device_id_type=MESH))
    each(nhead, lambda k: pl.semaphore_signal(barrier, inc=1, device_id={"head": head_peer(k)}, device_id_type=MESH))
    locals_ = [
        pltpu.make_async_copy(query_hbm, query, local_sem.at[0]),
        pltpu.make_async_copy(grad_hbm, grad, local_sem.at[1]),
        pltpu.make_async_copy(out_w, wo.at[g], local_sem.at[2]),
        pltpu.make_async_copy(key_w, kw.at[g], local_sem.at[3]),
        pltpu.make_async_copy(value_w, vw.at[g], local_sem.at[4]),
    ]
    for copy in locals_:
        copy.start()
    pl.semaphore_wait(barrier, ngroup + nhead - 2)

    def far_group(k):
        return lax.rem(chip + k, nchip) * 2 + core

    def from_group(k):
        return lax.rem(chip - k + nchip, nchip) * 2 + core

    def send_out_weight(k):
        remote(out_w, wo.at[g], wo_send, wo_recv.at[k], {"group": far_group(k)}).start()

    each(nchip, send_out_weight)
    remote(out_w, wo.at[g], wo_pass_send, wo_pass_recv, {"group": sibling}).start()

    bias = enc_bias[...]
    ctx = []
    for n in range(nheads):
        cols = slice(n * DK, (n + 1) * DK)
        scores = mm(qkv[0, :, cols], qkv[1, :, cols], 1, 1) * scale + bias
        e = jnp.exp(scores - jnp.max(scores, axis=1, keepdims=True))
        p = (e * (1.0 / jnp.sum(e, axis=1, keepdims=True))).astype(BF16)
        ctx.append(mm(p, qkv[2, :, cols], 1, 0).astype(BF16))
    ctx = jnp.concatenate(ctx, axis=1)

    def to_flat(x, ref, base):
        rows = x.shape[0]
        for c in range(chunks):
            ref[pl.ds(base * chunks + c, rows, stride=chunks), :] = x[:, c * LANES : (c + 1) * LANES]

    def from_flat(ref, base, rows, c):
        return ref[pl.ds(base * chunks + c, rows, stride=chunks), :]

    to_flat(resid[...].astype(F32), resid_flat, 0)

    def pass_out_weight(k):
        there = wo.at[from_group(k)]
        remote(there, there, wo_send, wo_recv.at[k], {"group": sibling}).wait_recv()
        remote(there, there, wo_pass_send, wo_pass_recv, {"group": sibling}).start()

    each(nchip, pass_out_weight)
    locals_[2].wait()
    total(wo.at[pl.ds(0, nchip)], wo_pass_send, wo_pass_recv).wait_recv()
    part = mm(ctx, wo[...].reshape(width, dim), 1, 0)

    to_flat(part, flat, 0)
    out_send[...] = flat[pl.ds(0, seq * chunks), :].reshape(nhead, blk, LANES).astype(BF16)

    def send_out(k):
        there = head_peer(k)
        remote(out_send.at[there], out_recv.at[k - 1], phase_send.at[0], phase_recv.at[0], {"head": there}).start()

    each(nhead, send_out)

    def send_kv(k):
        where = {"group": far_group(k)}
        remote(key_w, kw.at[g], kv_send, kv_recv.at[0, k], where).start()
        remote(value_w, vw.at[g], kv_send, kv_recv.at[1, k], where).start()

    each(nchip, send_kv)
    remote(key_w, kw.at[g], kv_pass_send, kv_pass_recv, {"group": sibling}).start()
    remote(value_w, vw.at[g], kv_pass_send, kv_pass_recv, {"group": sibling}).start()

    mine = pl.ds(pl.multiple_of(h * blk, blk), blk)
    memory = flat[mine, :] + resid_flat[mine, :]
    total(out_recv, phase_send.at[0], phase_recv.at[0]).wait_recv()
    memory = memory + jnp.sum(out_recv[...].astype(F32), axis=0)

    def row_mean(x):
        x3 = x.reshape(own_rows, chunks, LANES)
        m = jnp.sum(jnp.sum(x3, axis=1, keepdims=True), axis=2, keepdims=True) * (1.0 / dim)
        return jnp.broadcast_to(m, x3.shape).reshape(blk, LANES)

    gains = jnp.broadcast_to(gain[...][None], (own_rows, chunks, LANES)).reshape(blk, LANES)
    inv = lax.rsqrt(row_mean(memory * memory) + EPS)
    normed = memory * inv
    norm_all[g] = (normed * gains).astype(BF16)

    def send_norm(k):
        there = norm_all.at[g]
        remote(there, there, phase_send.at[1], phase_recv.at[1], {"group": group_peer(k)}).start()

    each(ngroup, send_norm)
    total(norm_all.at[pl.ds(0, ngroup - 1)], phase_send.at[1], phase_recv.at[1]).wait_recv()

    for s in range(mem):
        norm_pick[h, s * blk : (s + 1) * blk, :] = norm_all[sources[g, s]]

    def send_pick(k):
        there = norm_pick.at[h]
        remote(there, there, phase_send.at[2], phase_recv.at[2], {"head": head_peer(k)}).start()

    each(nhead, send_pick)

    def pass_kv(k):
        for i, ref in ((0, kw), (1, vw)):
            there = ref.at[from_group(k)]
            remote(there, there, kv_send, kv_recv.at[i, k], {"group": sibling}).wait_recv()
            remote(there, there, kv_pass_send, kv_pass_recv, {"group": sibling}).start()

    each(nchip, pass_kv)
    for i in (0, 1, 3, 4):
        locals_[i].wait()
    total(kw.at[pl.ds(0, 2 * nchip)], kv_pass_send, kv_pass_recv).wait_recv()
    total(norm_pick.at[pl.ds(0, nhead - 1)], phase_send.at[2], phase_recv.at[2]).wait_recv()
    for s in range(mem):
        rows = norm_pick[:, s * blk : (s + 1) * blk, :].astype(F32).reshape(seq * chunks, LANES)
        flat[pl.ds(s * seq * chunks, seq * chunks), :] = rows
    rows = mem * seq
    picked = jnp.concatenate([from_flat(flat, 0, rows, c).astype(BF16) for c in range(chunks)], axis=1)

    key_full = kw[...].reshape(dim, width)
    value_full = vw[...].reshape(dim, width)
    keys = mm(picked, key_full, 1, 0).astype(BF16)
    values = mm(picked, value_full, 1, 0).astype(BF16)
    cbias = cross_bias[...]
    qrows = query.shape[0]
    dks, dvs = [], []
    for n in range(nheads):
        cols = slice(n * DK, (n + 1) * DK)
        kept = keep[0, n].astype(F32)
        q_n, g_n = query[:, cols], grad[:, cols]
        k_n, v_n = keys[:, cols], values[:, cols]
        cross = (mm(k_n, q_n, 1, 1) * scale).reshape(mem, seq, qrows) + cbias[None]
        cross = cross.reshape(rows, qrows)
        e = jnp.exp(cross - jnp.max(cross, axis=0, keepdims=True))
        prob = e * (1.0 / jnp.sum(e, axis=0, keepdims=True))
        prob_low = prob.astype(BF16)
        context[:, cols] = (mm(prob_low, v_n, 0, 0) * kept).astype(BF16)
        dprob = mm(v_n, g_n, 1, 1)
        delta = jnp.sum(prob * dprob, axis=0, keepdims=True)
        dscore = (prob * (dprob - delta) * (scale * kept)).astype(BF16)
        dks.append(mm(dscore, q_n, 1, 0).astype(BF16))
        dvs.append((mm(prob_low, g_n, 1, 0) * kept).astype(BF16))
    context_copy = pltpu.make_async_copy(context, context_hbm, context_sem)
    context_copy.start()
    dks = jnp.concatenate(dks, axis=1)
    dvs = jnp.concatenate(dvs, axis=1)
    dnorm = mm(dks, key_full, 1, 1) + mm(dvs, value_full, 1, 1)

    to_flat(dnorm, flat, 0)
    for s in range(mem):
        block = flat[pl.ds(s * seq * chunks, seq * chunks), :].reshape(nhead, blk, LANES)
        dn_send[:, s * blk : (s + 1) * blk, :] = block.astype(BF16)

    def send_dn(k):
        there = head_peer(k)
        remote(dn_send.at[there], dn_recv.at[k - 1], phase_send.at[3], phase_recv.at[3], {"head": there}).start()

    each(nhead, send_dn)
    own = [flat[pl.ds(pl.multiple_of(s * seq * chunks + h * blk, blk), blk), :] for s in range(mem)]
    total(dn_recv, phase_send.at[3], phase_recv.at[3]).wait_recv()
    dn_all[g] = (jnp.concatenate(own, axis=0) + jnp.sum(dn_recv[...].astype(F32), axis=0)).astype(BF16)

    def send_all(k):
        there = dn_all.at[g]
        remote(there, there, phase_send.at[4], phase_recv.at[4], {"group": group_peer(k)}).start()

    each(ngroup, send_all)
    total(dn_all.at[pl.ds(0, ngroup - 1)], phase_send.at[4], phase_recv.at[4]).wait_recv()
    acc = jnp.zeros((blk, LANES), F32)
    for d in range(ngroup):
        for s in range(mem):
            block = dn_all[d, s * blk : (s + 1) * blk, :].astype(F32)
            acc = acc + block * (sources[d, s] == g).astype(F32)
    scaled = acc * gains
    mg_all[h] = (inv * (scaled - normed * row_mean(scaled * normed))).astype(BF16)

    def send_mg(k):
        there = mg_all.at[h]
        remote(there, there, phase_send.at[5], phase_recv.at[5], {"head": head_peer(k)}).start()

    each(nhead, send_mg)
    total(mg_all.at[pl.ds(0, nhead - 1)], phase_send.at[5], phase_recv.at[5]).wait_recv()
    flat[pl.ds(0, seq * chunks), :] = mg_all[...].astype(F32).reshape(seq * chunks, LANES)
    for c in range(chunks):
        memory_grad[:, c * LANES : (c + 1) * LANES] = from_flat(flat, 0, seq, c).astype(BF16)

    context_copy.wait()
    total(wo.at[pl.ds(0, nchip - 1)], wo_send, wo_recv.at[0]).wait_send()
    total(wo.at[pl.ds(0, nchip)], wo_pass_send, wo_pass_recv).wait_send()
    total(kw.at[pl.ds(0, 2 * nchip - 2)], kv_send, kv_recv.at[0, 0]).wait_send()
    total(kw.at[pl.ds(0, 2 * nchip)], kv_pass_send, kv_pass_recv).wait_send()
    for i, ref in enumerate((out_recv, norm_all.at[pl.ds(0, ngroup - 1)], norm_pick.at[pl.ds(0, nhead - 1)], dn_recv, dn_all.at[pl.ds(0, ngroup - 1)], mg_all.at[pl.ds(0, nhead - 1)])):
        total(ref, phase_send.at[i], phase_recv.at[i]).wait_send()


def shards(
    ngroup,
    nhead,
    enc_resid,
    enc_qkv,
    enc_bias,
    out_weight,
    final_gain,
    key_weight,
    value_weight,
    dec_query,
    cross_bias,
    out_grad,
    sources,
    head_keep,
):
    seq, dim = enc_resid.shape
    qrows, width = dec_query.shape
    mem = sources.shape[1]
    chunks = dim // LANES
    blk = seq // nhead * chunks
    nchip = ngroup // 2
    vmem = pl.BlockSpec(memory_space=pltpu.VMEM)
    smem = pl.BlockSpec(memory_space=pltpu.SMEM)
    anyw = pl.BlockSpec(memory_space=pl.ANY)
    dma = pltpu.SemaphoreType.DMA
    return tuple(
        pl.pallas_call(
            functools.partial(kernel, ngroup, nhead, mem),
            out_shape=(
                jax.ShapeDtypeStruct((qrows, width), BF16),
                jax.ShapeDtypeStruct((seq, dim), BF16),
            ),
            in_specs=[smem, smem, vmem, vmem, vmem, vmem, vmem, anyw, anyw, anyw, anyw, anyw],
            out_specs=(anyw, vmem),
            scratch_shapes=[
                pltpu.VMEM((ngroup,) + out_weight.shape, BF16),
                pltpu.VMEM((ngroup,) + key_weight.shape, BF16),
                pltpu.VMEM((ngroup,) + value_weight.shape, BF16),
                pltpu.VMEM((qrows, width), BF16),
                pltpu.VMEM((qrows, width), BF16),
                pltpu.VMEM((qrows, width), BF16),
                pltpu.VMEM((mem * seq * chunks, LANES), F32),
                pltpu.VMEM((seq * chunks, LANES), F32),
                pltpu.VMEM((nhead, blk, LANES), BF16),
                pltpu.VMEM((nhead - 1, blk, LANES), BF16),
                pltpu.VMEM((ngroup, blk, LANES), BF16),
                pltpu.VMEM((nhead, mem * blk, LANES), BF16),
                pltpu.VMEM((nhead, mem * blk, LANES), BF16),
                pltpu.VMEM((nhead - 1, mem * blk, LANES), BF16),
                pltpu.VMEM((ngroup, mem * blk, LANES), BF16),
                pltpu.VMEM((nhead, blk, LANES), BF16),
                dma((5,)),
                dma,
                dma,
                dma((nchip,)),
                dma,
                dma,
                dma,
                dma((2, nchip)),
                dma,
                dma,
                dma((6,)),
                dma((6,)),
            ],
            compiler_params=pltpu.CompilerParams(
                collective_id=0, has_side_effects=True, vmem_limit_bytes=40 * 1024 * 1024
            ),
        )(
            sources,
            head_keep,
            enc_resid,
            enc_qkv,
            enc_bias,
            final_gain.reshape(chunks, LANES),
            cross_bias.T,
            out_weight,
            key_weight,
            value_weight,
            dec_query,
            out_grad,
        )
    )


def solution(mesh):
    in_specs = (
        P("group", None),
        P(None, "group", "head"),
        P(),
        P(("head", "group"), None),
        P(),
        P("group", "head"),
        P("group", "head"),
        P("group", "head"),
        P(),
        P("group", "head"),
        P(),
        P("group", "head"),
    )
    out_specs = (P("group", "head"), P("group", None))
    step = functools.partial(shards, mesh.shape["group"], mesh.shape["head"])
    return jax.shard_map(step, mesh=mesh, in_specs=in_specs, out_specs=out_specs, check_vma=False)
```

time: 870 us -> 123 us (0.14)
  the two profiles are of different devices: /device:TPU:2 before, /device:TPU:4 now
where the time goes in v1:
time: 123 us
  Pallas kernels  112 us (91%)
  local copies, waits for them, and re-layouts  10.8 us (9%)
    pallas_call x1, Pallas kernels, shards(): pl.pallas_call(functools.partial(kernel, ngroup, nhead, mem), out_shape=(...  112 us
    unnamed x27, local copies, waits for them, and re-layouts  10.8 us

profile of v1, /device:TPU:4, one launch (start us, length us, event | category | flops | bytes accessed | tf_op | source)
XLA Modules:
  0.0 122.9 jit_solution(7085869866513622523)
XLA Ops:
  0.6 0.0 copy-start.11
  0.6 0.7 copy-done.11
  1.3 0.0 copy-start.9
  1.3 0.0 copy-start.10
  1.3 0.1 copy.14.sources
  1.4 0.6 copy-done.9
  2.0 0.0 copy-done.10
  2.0 0.0 copy-start
  2.0 1.0 copy-done
  3.0 0.0 copy-start.1
  3.0 1.0 copy-done.1
  4.0 0.0 copy-start.2
  4.0 0.9 copy-done.2
  4.9 0.0 copy-start.3
  4.9 0.9 copy-done.3
  5.8 0.0 copy-start.4
  5.8 0.9 copy-done.4
  6.7 0.0 copy-start.5
  6.7 0.8 copy-done.5
  7.6 0.0 copy-start.6
  7.6 0.8 copy-done.6
  8.4 0.0 copy-start.7
  8.4 0.8 copy-done.7
  9.2 0.0 copy-start.8
  9.2 0.8 copy-done.8
  10.0 111.5 %shard_map.131 = (bf16[384,512]{1,0:T(8,128)(2,1)S(1)}, bf16[64,1024]{1,0:T(8,128)(2,1)S(1)}) custom-call(s32[16,3]{1,0:T(8,128)S(1)} %copy.14.sources, s32[1,4]{1,0:T(1,128)S(1)} %copy-done.10, bf16[64,1024]{1,0:T(8,128)(2,1)S(1)} %copy-done.3, bf16[3,64,512]{2,1,0:T(8,128)(2,1)S(1)} %copy-done.2, f32[64,64]{1,0:T(8,128)S(1)} %copy-done.8, ...), custom_call_target="tpu_custom_call" | custom-call | tf_op jit(solution)/shard_map/pallas_call | solution.py:331
  121.5 0.7 copy.17
  122.3 0.7 copy.18
Async XLA Ops:
  0.6 0.7 copy-start.11
  1.3 0.7 copy-start.9
  1.3 0.7 copy-start.10
  2.0 1.0 copy-start
  3.0 1.0 copy-start.1
  4.0 0.9 copy-start.2
  4.9 0.9 copy-start.3
  5.8 0.9 copy-start.4
  6.7 0.8 copy-start.5
  7.6 0.8 copy-start.6
  8.4 0.8 copy-start.7
  9.2 0.8 copy-start.8

commit v2 on v1

--- a/solution.py
+++ b/solution.py
@@ -24,6 +24,20 @@
     ngroup,
     nhead,
     mem,
+    sources_hbm,
+    keep_hbm,
+    resid_hbm,
+    qkv_hbm,
+    enc_bias_hbm,
+    gain_hbm,
+    cross_bias_hbm,
+    out_w,
+    key_w,
+    value_w,
+    query_hbm,
+    grad_hbm,
+    context,
+    memory_grad,
     sources,
     keep,
     resid,
@@ -31,19 +45,11 @@
     enc_bias,
     gain,
     cross_bias,
-    out_w,
-    key_w,
-    value_w,
-    query_hbm,
-    grad_hbm,
-    context_hbm,
-    memory_grad,
     wo,
     kw,
     vw,
     query,
     grad,
-    context,
     flat,
     resid_flat,
     out_send,
@@ -51,11 +57,12 @@
     norm_all,
     norm_pick,
     dn_send,
-    dn_recv,
+    dn_near,
+    dn_sum,
+    dn_far,
     dn_all,
     mg_all,
     local_sem,
-    context_sem,
     wo_send,
     wo_recv,
     wo_pass_send,
@@ -64,6 +71,8 @@
     kv_recv,
     kv_pass_send,
     kv_pass_recv,
+    far_recv,
+    near_recv,
     phase_send,
     phase_recv,
 ):
@@ -81,14 +90,32 @@
     sibling = g + 1 - 2 * core
     nchip = ngroup // 2
 
+    nz, nx = nhead // 2, ngroup // 4
+    z, y = lax.div(h, 2), lax.rem(h, 2)
+    gx, gy = lax.div(g, 4), lax.rem(lax.div(g, 2), 2)
+
     def each(n, body):
         lax.fori_loop(1, n, lambda k, c: (body(k), c)[1], 0)
 
-    def group_peer(k):
-        return lax.rem(g + k, ngroup)
+    def head_at(dz, dy):
+        return lax.rem(z + dz + nz, nz) * 2 + lax.rem(y + dy, 2)
+
+    def group_at(dx, dy, dc):
+        return lax.rem(gx + dx, nx) * 4 + lax.rem(gy + dy, 2) * 2 + lax.rem(core + dc, 2)
 
     def head_peer(k):
-        return lax.rem(h + k, nhead)
+        j = lax.div(k - 1, 2)
+        away = nz // 2 - lax.div(j + 1, 2)
+        return head_at(away * (2 * lax.rem(j, 2) - 1), lax.rem(k, 2))
+
+    def spread(dx, dy, dc):
+        return -(min(dx, nx - dx) * 4 + dy * 4 + dc)
+
+    steps = [(dx, dy, dc) for dx in range(nx) for dy in range(2) for dc in range(2)][1:]
+    group_steps = sorted(steps, key=lambda t: spread(*t))
+    chip_steps = [(dx, dy) for dx, dy, dc in group_steps if dc == 0]
+    far_steps = sorted(range(2, nz, 4), key=lambda a: -min(a, nz - a))
+    near_steps = [(2, 1), (1, 1), (nz - 1, 1), (0, 1), (2, 0), (1, 0), (nz - 1, 0)]
 
     def remote(src, dst, send, recv, where):
         return pltpu.make_async_remote_copy(
@@ -104,7 +131,7 @@
         return remote(ref, ref, send, recv, {"group": sibling})
 
     barrier = pltpu.get_barrier_semaphore()
-    each(ngroup, lambda k: pl.semaphore_signal(barrier, inc=1, device_id={"group": group_peer(k)}, device_id_type=MESH))
+    each(ngroup, lambda k: pl.semaphore_signal(barrier, inc=1, device_id={"group": lax.rem(g + k, ngroup)}, device_id_type=MESH))
     each(nhead, lambda k: pl.semaphore_signal(barrier, inc=1, device_id={"head": head_peer(k)}, device_id_type=MESH))
     locals_ = [
         pltpu.make_async_copy(query_hbm, query, local_sem.at[0]),
@@ -112,23 +139,24 @@
         pltpu.make_async_copy(out_w, wo.at[g], local_sem.at[2]),
         pltpu.make_async_copy(key_w, kw.at[g], local_sem.at[3]),
         pltpu.make_async_copy(value_w, vw.at[g], local_sem.at[4]),
+        pltpu.make_async_copy(qkv_hbm, qkv, local_sem.at[5]),
+        pltpu.make_async_copy(enc_bias_hbm, enc_bias, local_sem.at[6]),
+        pltpu.make_async_copy(resid_hbm, resid, local_sem.at[7]),
+        pltpu.make_async_copy(gain_hbm, gain, local_sem.at[8]),
+        pltpu.make_async_copy(cross_bias_hbm, cross_bias, local_sem.at[9]),
+        pltpu.make_async_copy(sources_hbm, sources, local_sem.at[10]),
+        pltpu.make_async_copy(keep_hbm, keep, local_sem.at[11]),
     ]
     for copy in locals_:
         copy.start()
     pl.semaphore_wait(barrier, ngroup + nhead - 2)
 
-    def far_group(k):
-        return lax.rem(chip + k, nchip) * 2 + core
-
-    def from_group(k):
-        return lax.rem(chip - k + nchip, nchip) * 2 + core
-
-    def send_out_weight(k):
-        remote(out_w, wo.at[g], wo_send, wo_recv.at[k], {"group": far_group(k)}).start()
-
-    each(nchip, send_out_weight)
+    for i, (dx, dy) in enumerate(chip_steps):
+        remote(out_w, wo.at[g], wo_send, wo_recv.at[i], {"group": group_at(dx, dy, 0)}).start()
     remote(out_w, wo.at[g], wo_pass_send, wo_pass_recv, {"group": sibling}).start()
 
+    locals_[5].wait()
+    locals_[6].wait()
     bias = enc_bias[...]
     ctx = []
     for n in range(nheads):
@@ -147,14 +175,13 @@
     def from_flat(ref, base, rows, c):
         return ref[pl.ds(base * chunks + c, rows, stride=chunks), :]
 
+    locals_[7].wait()
     to_flat(resid[...].astype(F32), resid_flat, 0)
 
-    def pass_out_weight(k):
-        there = wo.at[from_group(k)]
-        remote(there, there, wo_send, wo_recv.at[k], {"group": sibling}).wait_recv()
+    for i, (dx, dy) in enumerate(chip_steps):
+        there = wo.at[group_at(nx - dx, dy, 0)]
+        remote(there, there, wo_send, wo_recv.at[i], {"group": sibling}).wait_recv()
         remote(there, there, wo_pass_send, wo_pass_recv, {"group": sibling}).start()
-
-    each(nchip, pass_out_weight)
     locals_[2].wait()
     total(wo.at[pl.ds(0, nchip)], wo_pass_send, wo_pass_recv).wait_recv()
     part = mm(ctx, wo[...].reshape(width, dim), 1, 0)
@@ -168,12 +195,10 @@
 
     each(nhead, send_out)
 
-    def send_kv(k):
-        where = {"group": far_group(k)}
-        remote(key_w, kw.at[g], kv_send, kv_recv.at[0, k], where).start()
-        remote(value_w, vw.at[g], kv_send, kv_recv.at[1, k], where).start()
-
-    each(nchip, send_kv)
+    for i, (dx, dy) in enumerate(chip_steps):
+        where = {"group": group_at(dx, dy, 0)}
+        remote(key_w, kw.at[g], kv_send, kv_recv.at[0, i], where).start()
+        remote(value_w, vw.at[g], kv_send, kv_recv.at[1, i], where).start()
     remote(key_w, kw.at[g], kv_pass_send, kv_pass_recv, {"group": sibling}).start()
     remote(value_w, vw.at[g], kv_pass_send, kv_pass_recv, {"group": sibling}).start()
 
@@ -187,38 +212,43 @@
         m = jnp.sum(jnp.sum(x3, axis=1, keepdims=True), axis=2, keepdims=True) * (1.0 / dim)
         return jnp.broadcast_to(m, x3.shape).reshape(blk, LANES)
 
+    locals_[8].wait()
     gains = jnp.broadcast_to(gain[...][None], (own_rows, chunks, LANES)).reshape(blk, LANES)
     inv = lax.rsqrt(row_mean(memory * memory) + EPS)
     normed = memory * inv
     norm_all[g] = (normed * gains).astype(BF16)
 
-    def send_norm(k):
-        there = norm_all.at[g]
-        remote(there, there, phase_send.at[1], phase_recv.at[1], {"group": group_peer(k)}).start()
-
-    each(ngroup, send_norm)
+    there = norm_all.at[g]
+    for step in group_steps:
+        remote(there, there, phase_send.at[1], phase_recv.at[1], {"group": group_at(*step)}).start()
     total(norm_all.at[pl.ds(0, ngroup - 1)], phase_send.at[1], phase_recv.at[1]).wait_recv()
 
+    locals_[10].wait()
     for s in range(mem):
-        norm_pick[h, s * blk : (s + 1) * blk, :] = norm_all[sources[g, s]]
-
-    def send_pick(k):
-        there = norm_pick.at[h]
-        remote(there, there, phase_send.at[2], phase_recv.at[2], {"head": head_peer(k)}).start()
-
-    each(nhead, send_pick)
-
-    def pass_kv(k):
-        for i, ref in ((0, kw), (1, vw)):
-            there = ref.at[from_group(k)]
-            remote(there, there, kv_send, kv_recv.at[i, k], {"group": sibling}).wait_recv()
+        norm_pick[h, s * blk : (s + 1) * blk, :] = norm_all[sources[s, g]]
+
+    there = norm_pick.at[h]
+    for i, a in enumerate(far_steps):
+        remote(there, there, phase_send.at[2], far_recv.at[i], {"head": head_at(a, 0)}).start()
+
+    for i, (dx, dy) in enumerate(chip_steps):
+        for j, ref in ((0, kw), (1, vw)):
+            there = ref.at[group_at(nx - dx, dy, 0)]
+            remote(there, there, kv_send, kv_recv.at[j, i], {"group": sibling}).wait_recv()
             remote(there, there, kv_pass_send, kv_pass_recv, {"group": sibling}).start()
 
-    each(nchip, pass_kv)
-    for i in (0, 1, 3, 4):
+    nfar = len(far_steps)
+    npass = nfar * len(near_steps) - 1
+    for i, a in reversed(list(enumerate(far_steps))):
+        there = norm_pick.at[head_at(nz - a, 0)]
+        remote(there, there, phase_send.at[2], far_recv.at[i], {"head": head_at(a, 0)}).wait_recv()
+        for b, dy in near_steps:
+            if (a + b) % nz or dy:
+                remote(there, there, phase_send.at[6], phase_recv.at[2], {"head": head_at(b, dy)}).start()
+    for i in (0, 1, 3, 4, 9, 11):
         locals_[i].wait()
     total(kw.at[pl.ds(0, 2 * nchip)], kv_pass_send, kv_pass_recv).wait_recv()
-    total(norm_pick.at[pl.ds(0, nhead - 1)], phase_send.at[2], phase_recv.at[2]).wait_recv()
+    total(norm_pick.at[pl.ds(0, npass)], phase_send.at[6], phase_recv.at[2]).wait_recv()
     for s in range(mem):
         rows = norm_pick[:, s * blk : (s + 1) * blk, :].astype(F32).reshape(seq * chunks, LANES)
         flat[pl.ds(s * seq * chunks, seq * chunks), :] = rows
@@ -248,8 +278,6 @@
         dscore = (prob * (dprob - delta) * (scale * kept)).astype(BF16)
         dks.append(mm(dscore, q_n, 1, 0).astype(BF16))
         dvs.append((mm(prob_low, g_n, 1, 0) * kept).astype(BF16))
-    context_copy = pltpu.make_async_copy(context, context_hbm, context_sem)
-    context_copy.start()
     dks = jnp.concatenate(dks, axis=1)
     dvs = jnp.concatenate(dvs, axis=1)
     dnorm = mm(dks, key_full, 1, 1) + mm(dvs, value_full, 1, 1)
@@ -259,26 +287,27 @@
         block = flat[pl.ds(s * seq * chunks, seq * chunks), :].reshape(nhead, blk, LANES)
         dn_send[:, s * blk : (s + 1) * blk, :] = block.astype(BF16)
 
-    def send_dn(k):
-        there = head_peer(k)
-        remote(dn_send.at[there], dn_recv.at[k - 1], phase_send.at[3], phase_recv.at[3], {"head": there}).start()
-
-    each(nhead, send_dn)
-    own = [flat[pl.ds(pl.multiple_of(s * seq * chunks + h * blk, blk), blk), :] for s in range(mem)]
-    total(dn_recv, phase_send.at[3], phase_recv.at[3]).wait_recv()
-    dn_all[g] = (jnp.concatenate(own, axis=0) + jnp.sum(dn_recv[...].astype(F32), axis=0)).astype(BF16)
-
-    def send_all(k):
-        there = dn_all.at[g]
-        remote(there, there, phase_send.at[4], phase_recv.at[4], {"group": group_peer(k)}).start()
-
-    each(ngroup, send_all)
+    for i, a in enumerate(far_steps):
+        for j, (b, dy) in enumerate(near_steps):
+            there = dn_send.at[head_at(a + b, dy)]
+            remote(there, dn_near.at[i, j], phase_send.at[3], near_recv.at[i], {"head": head_at(b, dy)}).start()
+    for i, a in enumerate(far_steps):
+        total(dn_near.at[i], phase_send.at[3], near_recv.at[i]).wait_recv()
+        near = dn_send[head_at(a, 0)].astype(F32) + jnp.sum(dn_near[i].astype(F32), axis=0)
+        dn_sum[i] = near.astype(BF16)
+        remote(dn_sum.at[i], dn_far.at[i], phase_send.at[7], phase_recv.at[3], {"head": head_at(a, 0)}).start()
+    total(dn_far, phase_send.at[7], phase_recv.at[3]).wait_recv()
+    dn_all[g] = jnp.sum(dn_far[...].astype(F32), axis=0).astype(BF16)
+
+    there = dn_all.at[g]
+    for step in group_steps:
+        remote(there, there, phase_send.at[4], phase_recv.at[4], {"group": group_at(*step)}).start()
     total(dn_all.at[pl.ds(0, ngroup - 1)], phase_send.at[4], phase_recv.at[4]).wait_recv()
     acc = jnp.zeros((blk, LANES), F32)
     for d in range(ngroup):
         for s in range(mem):
             block = dn_all[d, s * blk : (s + 1) * blk, :].astype(F32)
-            acc = acc + block * (sources[d, s] == g).astype(F32)
+            acc = acc + block * (sources[s, d] == g).astype(F32)
     scaled = acc * gains
     mg_all[h] = (inv * (scaled - normed * row_mean(scaled * normed))).astype(BF16)
 
@@ -292,13 +321,22 @@
     for c in range(chunks):
         memory_grad[:, c * LANES : (c + 1) * LANES] = from_flat(flat, 0, seq, c).astype(BF16)
 
-    context_copy.wait()
     total(wo.at[pl.ds(0, nchip - 1)], wo_send, wo_recv.at[0]).wait_send()
     total(wo.at[pl.ds(0, nchip)], wo_pass_send, wo_pass_recv).wait_send()
     total(kw.at[pl.ds(0, 2 * nchip - 2)], kv_send, kv_recv.at[0, 0]).wait_send()
     total(kw.at[pl.ds(0, 2 * nchip)], kv_pass_send, kv_pass_recv).wait_send()
-    for i, ref in enumerate((out_recv, norm_all.at[pl.ds(0, ngroup - 1)], norm_pick.at[pl.ds(0, nhead - 1)], dn_recv, dn_all.at[pl.ds(0, ngroup - 1)], mg_all.at[pl.ds(0, nhead - 1)])):
-        total(ref, phase_send.at[i], phase_recv.at[i]).wait_send()
+    sent = (
+        out_recv,
+        norm_all.at[pl.ds(0, ngroup - 1)],
+        norm_pick.at[pl.ds(0, nfar)],
+        dn_near,
+        dn_all.at[pl.ds(0, ngroup - 1)],
+        mg_all.at[pl.ds(0, nhead - 1)],
+        norm_pick.at[pl.ds(0, npass)],
+        dn_far,
+    )
+    for i, ref in enumerate(sent):
+        total(ref, phase_send.at[i], phase_recv.at[0]).wait_send()
 
 
 def shards(
@@ -323,24 +361,44 @@
     chunks = dim // LANES
     blk = seq // nhead * chunks
     nchip = ngroup // 2
+    nfar = nhead // 8
     vmem = pl.BlockSpec(memory_space=pltpu.VMEM)
-    smem = pl.BlockSpec(memory_space=pltpu.SMEM)
-    anyw = pl.BlockSpec(memory_space=pl.ANY)
+    hbm = pl.BlockSpec(memory_space=pltpu.HBM)
     dma = pltpu.SemaphoreType.DMA
+    operands = (
+        sources.T,
+        head_keep,
+        enc_resid,
+        enc_qkv,
+        enc_bias,
+        final_gain.reshape(chunks, LANES),
+        cross_bias.T,
+        out_weight,
+        key_weight,
+        value_weight,
+        dec_query,
+        out_grad,
+    )
     return tuple(
         pl.pallas_call(
             functools.partial(kernel, ngroup, nhead, mem),
             out_shape=(
-                jax.ShapeDtypeStruct((qrows, width), BF16),
-                jax.ShapeDtypeStruct((seq, dim), BF16),
+                pltpu.VMEM((qrows, width), BF16),
+                pltpu.VMEM((seq, dim), BF16),
             ),
-            in_specs=[smem, smem, vmem, vmem, vmem, vmem, vmem, anyw, anyw, anyw, anyw, anyw],
-            out_specs=(anyw, vmem),
+            in_specs=[hbm] * 12,
+            out_specs=(vmem, vmem),
             scratch_shapes=[
+                pltpu.SMEM(sources.shape[::-1], jnp.int32),
+                pltpu.SMEM(head_keep.shape, jnp.int32),
+                pltpu.VMEM(enc_resid.shape, BF16),
+                pltpu.VMEM(enc_qkv.shape, BF16),
+                pltpu.VMEM(enc_bias.shape, F32),
+                pltpu.VMEM((chunks, LANES), F32),
+                pltpu.VMEM(cross_bias.shape[::-1], F32),
                 pltpu.VMEM((ngroup,) + out_weight.shape, BF16),
                 pltpu.VMEM((ngroup,) + key_weight.shape, BF16),
                 pltpu.VMEM((ngroup,) + value_weight.shape, BF16),
-                pltpu.VMEM((qrows, width), BF16),
                 pltpu.VMEM((qrows, width), BF16),
                 pltpu.VMEM((qrows, width), BF16),
                 pltpu.VMEM((mem * seq * chunks, LANES), F32),
@@ -350,11 +408,12 @@
                 pltpu.VMEM((ngroup, blk, LANES), BF16),
                 pltpu.VMEM((nhead, mem * blk, LANES), BF16),
                 pltpu.VMEM((nhead, mem * blk, LANES), BF16),
-                pltpu.VMEM((nhead - 1, mem * blk, LANES), BF16),
+                pltpu.VMEM((nfar, 7, mem * blk, LANES), BF16),
+                pltpu.VMEM((nfar, mem * blk, LANES), BF16),
+                pltpu.VMEM((nfar, mem * blk, LANES), BF16),
                 pltpu.VMEM((ngroup, mem * blk, LANES), BF16),
                 pltpu.VMEM((nhead, blk, LANES), BF16),
-                dma((5,)),
-                dma,
+                dma((12,)),
                 dma,
                 dma((nchip,)),
                 dma,
@@ -363,25 +422,16 @@
                 dma((2, nchip)),
                 dma,
                 dma,
-                dma((6,)),
+                dma((nfar,)),
+                dma((nfar,)),
+                dma((8,)),
                 dma((6,)),
             ],
             compiler_params=pltpu.CompilerParams(
                 collective_id=0, has_side_effects=True, vmem_limit_bytes=40 * 1024 * 1024
             ),
         )(
-            sources,
-            head_keep,
-            enc_resid,
-            enc_qkv,
-            enc_bias,
-            final_gain.reshape(chunks, LANES),
-            cross_bias.T,
-            out_weight,
-            key_weight,
-            value_weight,
-            dec_query,
-            out_grad,
+            *(pltpu.with_memory_space_constraint(x, pltpu.HBM) for x in operands),
         )
     )
 

time: 123 us -> 91.2 us (0.74)
  the two profiles are of different devices: /device:TPU:4 before, /device:TPU:1 now
where the time goes in v2:
time: 91.2 us; the launch traced here: 91.1 us
  Pallas kernels  89 us (98%)
  local copies, waits for them, and re-layouts  1.4 us (2%)
    pallas_call x1, Pallas kernels, shards(): pl.pallas_call(functools.partial(kernel, ngroup, nhead, mem), out_shape=(...  89 us

profile of v2, /device:TPU:1, one launch (start us, length us, event | category | flops | bytes accessed | tf_op | source)
XLA Modules:
  0.0 91.1 jit_solution(14739975266468052858)
XLA Ops:
  0.6 89.0 %shard_map.131 = (bf16[384,512]{1,0:T(8,128)(2,1)S(1)}, bf16[64,1024]{1,0:T(8,128)(2,1)S(1)}) custom-call(s32[3,16]{1,0:T(4,128)} %bitcast.5, s32[1,4]{1,0:T(1,128)} %keep_hbm.1, bf16[64,1024]{1,0:T(8,128)(2,1)} %resid_hbm.1, bf16[3,64,512]{2,1,0:T(8,128)(2,1)} %qkv_hbm.1, f32[64,64]{1,0:T(8,128)} %enc_bias_hbm.1, f32[8,128]{1,0:T(8,128)} %bitcast.4, ...), custom_call_target="tpu_custom_call" | custom-call | tf_op jit(solution)/shard_map/pallas_call | solution.py:383
  89.7 0.7 copy.16
  90.4 0.7 copy.17

commit v3 on v2

--- a/solution.py
+++ b/solution.py
@@ -75,6 +75,7 @@
     near_recv,
     phase_send,
     phase_recv,
+    ready,
 ):
     seq, dim = resid.shape
     width = query.shape[1]
@@ -131,8 +132,17 @@
         return remote(ref, ref, send, recv, {"group": sibling})
 
     barrier = pltpu.get_barrier_semaphore()
-    each(ngroup, lambda k: pl.semaphore_signal(barrier, inc=1, device_id={"group": lax.rem(g + k, ngroup)}, device_id_type=MESH))
-    each(nhead, lambda k: pl.semaphore_signal(barrier, inc=1, device_id={"head": head_peer(k)}, device_id_type=MESH))
+    even, odd = g - core, g - core + 1
+
+    def hello(**where):
+        pl.semaphore_signal(barrier, inc=1, device_id=where, device_id_type=MESH)
+
+    def tell_sibling():
+        pl.semaphore_signal(ready, inc=1, device_id={"group": sibling}, device_id_type=MESH)
+
+    each(nchip, lambda k: hello(group=lax.rem(chip + k, nchip) * 2))
+    pl.when(core == 1)(lambda: hello(group=even))
+    each(nhead, lambda k: hello(group=odd, head=head_peer(k)))
     locals_ = [
         pltpu.make_async_copy(query_hbm, query, local_sem.at[0]),
         pltpu.make_async_copy(grad_hbm, grad, local_sem.at[1]),
@@ -149,7 +159,15 @@
     ]
     for copy in locals_:
         copy.start()
-    pl.semaphore_wait(barrier, ngroup + nhead - 2)
+
+    @pl.when(core == 0)
+    def _():
+        pl.semaphore_wait(barrier, ngroup - 1)
+        tell_sibling()
+
+    @pl.when(core == 1)
+    def _():
+        pl.semaphore_wait(ready, 1)
 
     for i, (dx, dy) in enumerate(chip_steps):
         remote(out_w, wo.at[g], wo_send, wo_recv.at[i], {"group": group_at(dx, dy, 0)}).start()
@@ -182,6 +200,12 @@
         there = wo.at[group_at(nx - dx, dy, 0)]
         remote(there, there, wo_send, wo_recv.at[i], {"group": sibling}).wait_recv()
         remote(there, there, wo_pass_send, wo_pass_recv, {"group": sibling}).start()
+
+    @pl.when(core == 1)
+    def _():
+        pl.semaphore_wait(barrier, 2 * (nhead - 1))
+        tell_sibling()
+
     locals_[2].wait()
     total(wo.at[pl.ds(0, nchip)], wo_pass_send, wo_pass_recv).wait_recv()
     part = mm(ctx, wo[...].reshape(width, dim), 1, 0)
@@ -192,6 +216,10 @@
     def send_out(k):
         there = head_peer(k)
         remote(out_send.at[there], out_recv.at[k - 1], phase_send.at[0], phase_recv.at[0], {"head": there}).start()
+
+    @pl.when(core == 0)
+    def _():
+        pl.semaphore_wait(ready, 1)
 
     each(nhead, send_out)
 
@@ -426,6 +454,7 @@
                 dma((nfar,)),
                 dma((8,)),
                 dma((6,)),
+                pltpu.SemaphoreType.REGULAR,
             ],
             compiler_params=pltpu.CompilerParams(
                 collective_id=0, has_side_effects=True, vmem_limit_bytes=40 * 1024 * 1024

time: 91.2 us -> 87.3 us (0.957)
  Pallas kernels: 89 us -> 85.2 us
    pallas_call x1, Pallas kernels: 89 us -> 85.2 us  [shards(): pl.pallas_call(functools.partial(kernel, ngroup, nhead, mem), out_shape=(...]
where the time goes in v3:
time: 87.3 us; the launch traced here: 87.2 us
  Pallas kernels  85.2 us (98%)
  local copies, waits for them, and re-layouts  1.4 us (2%)
    pallas_call x1, Pallas kernels, shards(): pl.pallas_call(functools.partial(kernel, ngroup, nhead, mem), out_shape=(...  85.2 us

profile of v3, /device:TPU:1, one launch (start us, length us, event | category | flops | bytes accessed | tf_op | source)
XLA Modules:
  0.0 87.2 jit_solution(11641595594156466374)
XLA Ops:
  0.6 85.2 %shard_map.131 = (bf16[384,512]{1,0:T(8,128)(2,1)S(1)}, bf16[64,1024]{1,0:T(8,128)(2,1)S(1)}) custom-call(s32[3,16]{1,0:T(4,128)} %bitcast.5, s32[1,4]{1,0:T(1,128)} %keep_hbm.1, bf16[64,1024]{1,0:T(8,128)(2,1)} %resid_hbm.1, bf16[3,64,512]{2,1,0:T(8,128)(2,1)} %qkv_hbm.1, f32[64,64]{1,0:T(8,128)} %enc_bias_hbm.1, f32[8,128]{1,0:T(8,128)} %bitcast.4, ...), custom_call_target="tpu_custom_call" | custom-call | tf_op jit(solution)/shard_map/pallas_call | solution.py:411
  85.8 0.7 copy.16
  86.6 0.7 copy.17

commit v4 on v3

--- a/solution.py
+++ b/solution.py
@@ -60,7 +60,10 @@
     dn_near,
     dn_sum,
     dn_far,
-    dn_all,
+    probs,
+    pick,
+    dn_out,
+    dn_in,
     mg_all,
     local_sem,
     wo_send,
@@ -104,6 +107,10 @@
     def group_at(dx, dy, dc):
         return lax.rem(gx + dx, nx) * 4 + lax.rem(gy + dy, 2) * 2 + lax.rem(core + dc, 2)
 
+    head_steps = sorted(
+        [(dz, dy) for dz in range(nz) for dy in range(2)][1:], key=lambda t: -(min(t[0], nz - t[0]) * 2 + t[1])
+    )
+
     def head_peer(k):
         j = lax.div(k - 1, 2)
         away = nz // 2 - lax.div(j + 1, 2)
@@ -196,6 +203,12 @@
     locals_[7].wait()
     to_flat(resid[...].astype(F32), resid_flat, 0)
 
+    locals_[10].wait()
+    for e in range(ngroup):
+        for s in range(mem):
+            reads = (sources[s, g] == e).astype(jnp.int32)
+            pick[e * mem + s] = jnp.full((blk, LANES), reads, jnp.int32).astype(F32)
+
     for i, (dx, dy) in enumerate(chip_steps):
         there = wo.at[group_at(nx - dx, dy, 0)]
         remote(there, there, wo_send, wo_recv.at[i], {"group": sibling}).wait_recv()
@@ -213,22 +226,17 @@
     to_flat(part, flat, 0)
     out_send[...] = flat[pl.ds(0, seq * chunks), :].reshape(nhead, blk, LANES).astype(BF16)
 
-    def send_out(k):
-        there = head_peer(k)
-        remote(out_send.at[there], out_recv.at[k - 1], phase_send.at[0], phase_recv.at[0], {"head": there}).start()
-
     @pl.when(core == 0)
     def _():
         pl.semaphore_wait(ready, 1)
 
-    each(nhead, send_out)
+    for i, step in enumerate(head_steps):
+        there = head_at(*step)
+        remote(out_send.at[there], out_recv.at[i], phase_send.at[0], phase_recv.at[0], {"head": there}).start()
 
     for i, (dx, dy) in enumerate(chip_steps):
-        where = {"group": group_at(dx, dy, 0)}
-        remote(key_w, kw.at[g], kv_send, kv_recv.at[0, i], where).start()
-        remote(value_w, vw.at[g], kv_send, kv_recv.at[1, i], where).start()
-    remote(key_w, kw.at[g], kv_pass_send, kv_pass_recv, {"group": sibling}).start()
-    remote(value_w, vw.at[g], kv_pass_send, kv_pass_recv, {"group": sibling}).start()
+        remote(key_w, kw.at[g], kv_send, kv_recv.at[0, i], {"group": group_at(dx, dy, 0)}).start()
+    remote(key_w, kw.at[g], kv_pass_send, kv_pass_recv.at[0], {"group": sibling}).start()
 
     mine = pl.ds(pl.multiple_of(h * blk, blk), blk)
     memory = flat[mine, :] + resid_flat[mine, :]
@@ -251,19 +259,23 @@
         remote(there, there, phase_send.at[1], phase_recv.at[1], {"group": group_at(*step)}).start()
     total(norm_all.at[pl.ds(0, ngroup - 1)], phase_send.at[1], phase_recv.at[1]).wait_recv()
 
-    locals_[10].wait()
     for s in range(mem):
         norm_pick[h, s * blk : (s + 1) * blk, :] = norm_all[sources[s, g]]
 
     there = norm_pick.at[h]
     for i, a in enumerate(far_steps):
         remote(there, there, phase_send.at[2], far_recv.at[i], {"head": head_at(a, 0)}).start()
-
     for i, (dx, dy) in enumerate(chip_steps):
-        for j, ref in ((0, kw), (1, vw)):
+        remote(value_w, vw.at[g], kv_send, kv_recv.at[1, i], {"group": group_at(dx, dy, 0)}).start()
+    remote(value_w, vw.at[g], kv_pass_send, kv_pass_recv.at[1], {"group": sibling}).start()
+
+    def pass_kv(j, ref):
+        for i, (dx, dy) in enumerate(chip_steps):
             there = ref.at[group_at(nx - dx, dy, 0)]
             remote(there, there, kv_send, kv_recv.at[j, i], {"group": sibling}).wait_recv()
-            remote(there, there, kv_pass_send, kv_pass_recv, {"group": sibling}).start()
+            remote(there, there, kv_pass_send, kv_pass_recv.at[j], {"group": sibling}).start()
+
+    pass_kv(0, kw)
 
     nfar = len(far_steps)
     npass = nfar * len(near_steps) - 1
@@ -273,9 +285,10 @@
         for b, dy in near_steps:
             if (a + b) % nz or dy:
                 remote(there, there, phase_send.at[6], phase_recv.at[2], {"head": head_at(b, dy)}).start()
-    for i in (0, 1, 3, 4, 9, 11):
+    pass_kv(1, vw)
+    for i in (0, 3, 9, 11):
         locals_[i].wait()
-    total(kw.at[pl.ds(0, 2 * nchip)], kv_pass_send, kv_pass_recv).wait_recv()
+    total(kw.at[pl.ds(0, nchip)], kv_pass_send, kv_pass_recv.at[0]).wait_recv()
     total(norm_pick.at[pl.ds(0, npass)], phase_send.at[6], phase_recv.at[2]).wait_recv()
     for s in range(mem):
         rows = norm_pick[:, s * blk : (s + 1) * blk, :].astype(F32).reshape(seq * chunks, LANES)
@@ -284,21 +297,27 @@
     picked = jnp.concatenate([from_flat(flat, 0, rows, c).astype(BF16) for c in range(chunks)], axis=1)
 
     key_full = kw[...].reshape(dim, width)
-    value_full = vw[...].reshape(dim, width)
     keys = mm(picked, key_full, 1, 0).astype(BF16)
-    values = mm(picked, value_full, 1, 0).astype(BF16)
     cbias = cross_bias[...]
     qrows = query.shape[0]
+    for n in range(nheads):
+        cols = slice(n * DK, (n + 1) * DK)
+        cross = (mm(keys[:, cols], query[:, cols], 1, 1) * scale).reshape(mem, seq, qrows) + cbias[None]
+        cross = cross.reshape(rows, qrows)
+        e = jnp.exp(cross - jnp.max(cross, axis=0, keepdims=True))
+        probs[n] = e * (1.0 / jnp.sum(e, axis=0, keepdims=True))
+
+    locals_[1].wait()
+    locals_[4].wait()
+    total(vw.at[pl.ds(0, nchip)], kv_pass_send, kv_pass_recv.at[1]).wait_recv()
+    value_full = vw[...].reshape(dim, width)
+    values = mm(picked, value_full, 1, 0).astype(BF16)
     dks, dvs = [], []
     for n in range(nheads):
         cols = slice(n * DK, (n + 1) * DK)
         kept = keep[0, n].astype(F32)
-        q_n, g_n = query[:, cols], grad[:, cols]
-        k_n, v_n = keys[:, cols], values[:, cols]
-        cross = (mm(k_n, q_n, 1, 1) * scale).reshape(mem, seq, qrows) + cbias[None]
-        cross = cross.reshape(rows, qrows)
-        e = jnp.exp(cross - jnp.max(cross, axis=0, keepdims=True))
-        prob = e * (1.0 / jnp.sum(e, axis=0, keepdims=True))
+        q_n, g_n, v_n = query[:, cols], grad[:, cols], values[:, cols]
+        prob = probs[n]
         prob_low = prob.astype(BF16)
         context[:, cols] = (mm(prob_low, v_n, 0, 0) * kept).astype(BF16)
         dprob = mm(v_n, g_n, 1, 1)
@@ -325,25 +344,25 @@
         dn_sum[i] = near.astype(BF16)
         remote(dn_sum.at[i], dn_far.at[i], phase_send.at[7], phase_recv.at[3], {"head": head_at(a, 0)}).start()
     total(dn_far, phase_send.at[7], phase_recv.at[3]).wait_recv()
-    dn_all[g] = jnp.sum(dn_far[...].astype(F32), axis=0).astype(BF16)
-
-    there = dn_all.at[g]
-    for step in group_steps:
-        remote(there, there, phase_send.at[4], phase_recv.at[4], {"group": group_at(*step)}).start()
-    total(dn_all.at[pl.ds(0, ngroup - 1)], phase_send.at[4], phase_recv.at[4]).wait_recv()
-    acc = jnp.zeros((blk, LANES), F32)
-    for d in range(ngroup):
+    dn_sum_all = jnp.sum(dn_far[...].astype(F32), axis=0)
+
+    for e in range(ngroup):
+        acc = jnp.zeros((blk, LANES), F32)
         for s in range(mem):
-            block = dn_all[d, s * blk : (s + 1) * blk, :].astype(F32)
-            acc = acc + block * (sources[s, d] == g).astype(F32)
+            acc = acc + dn_sum_all[s * blk : (s + 1) * blk] * pick[e * mem + s]
+        dn_out[e] = acc.astype(BF16)
+    for i, step in enumerate(group_steps):
+        there = group_at(*step)
+        remote(dn_out.at[there], dn_in.at[i], phase_send.at[4], phase_recv.at[4], {"group": there}).start()
+    acc = dn_out[g].astype(F32)
+    total(dn_in, phase_send.at[4], phase_recv.at[4]).wait_recv()
+    acc = acc + jnp.sum(dn_in[...].astype(F32), axis=0)
     scaled = acc * gains
     mg_all[h] = (inv * (scaled - normed * row_mean(scaled * normed))).astype(BF16)
 
-    def send_mg(k):
-        there = mg_all.at[h]
-        remote(there, there, phase_send.at[5], phase_recv.at[5], {"head": head_peer(k)}).start()
-
-    each(nhead, send_mg)
+    there = mg_all.at[h]
+    for step in head_steps:
+        remote(there, there, phase_send.at[5], phase_recv.at[5], {"head": head_at(*step)}).start()
     total(mg_all.at[pl.ds(0, nhead - 1)], phase_send.at[5], phase_recv.at[5]).wait_recv()
     flat[pl.ds(0, seq * chunks), :] = mg_all[...].astype(F32).reshape(seq * chunks, LANES)
     for c in range(chunks):
@@ -352,19 +371,30 @@
     total(wo.at[pl.ds(0, nchip - 1)], wo_send, wo_recv.at[0]).wait_send()
     total(wo.at[pl.ds(0, nchip)], wo_pass_send, wo_pass_recv).wait_send()
     total(kw.at[pl.ds(0, 2 * nchip - 2)], kv_send, kv_recv.at[0, 0]).wait_send()
-    total(kw.at[pl.ds(0, 2 * nchip)], kv_pass_send, kv_pass_recv).wait_send()
+    total(kw.at[pl.ds(0, 2 * nchip)], kv_pass_send, kv_pass_recv.at[0]).wait_send()
     sent = (
         out_recv,
         norm_all.at[pl.ds(0, ngroup - 1)],
         norm_pick.at[pl.ds(0, nfar)],
         dn_near,
-        dn_all.at[pl.ds(0, ngroup - 1)],
+        dn_in,
         mg_all.at[pl.ds(0, nhead - 1)],
         norm_pick.at[pl.ds(0, npass)],
         dn_far,
     )
     for i, ref in enumerate(sent):
         total(ref, phase_send.at[i], phase_recv.at[0]).wait_send()
+
+
+def store(context, memory_grad, context_hbm, memory_grad_hbm, sem):
+    copies = (
+        pltpu.make_async_copy(context, context_hbm, sem.at[0]),
+        pltpu.make_async_copy(memory_grad, memory_grad_hbm, sem.at[1]),
+    )
+    for copy in copies:
+        copy.start()
+    for copy in copies:
+        copy.wait()
 
 
 def shards(
@@ -407,61 +437,71 @@
         dec_query,
         out_grad,
     )
+    held = pl.pallas_call(
+        functools.partial(kernel, ngroup, nhead, mem),
+        out_shape=(
+            pltpu.VMEM((qrows, width), BF16),
+            pltpu.VMEM((seq, dim), BF16),
+        ),
+        in_specs=[hbm] * 12,
+        out_specs=(vmem, vmem),
+        scratch_shapes=[
+            pltpu.SMEM(sources.shape[::-1], jnp.int32),
+            pltpu.SMEM(head_keep.shape, jnp.int32),
+            pltpu.VMEM(enc_resid.shape, BF16),
+            pltpu.VMEM(enc_qkv.shape, BF16),
+            pltpu.VMEM(enc_bias.shape, F32),
+            pltpu.VMEM((chunks, LANES), F32),
+            pltpu.VMEM(cross_bias.shape[::-1], F32),
+            pltpu.VMEM((ngroup,) + out_weight.shape, BF16),
+            pltpu.VMEM((ngroup,) + key_weight.shape, BF16),
+            pltpu.VMEM((ngroup,) + value_weight.shape, BF16),
+            pltpu.VMEM((qrows, width), BF16),
+            pltpu.VMEM((qrows, width), BF16),
+            pltpu.VMEM((mem * seq * chunks, LANES), F32),
+            pltpu.VMEM((seq * chunks, LANES), F32),
+            pltpu.VMEM((nhead, blk, LANES), BF16),
+            pltpu.VMEM((nhead - 1, blk, LANES), BF16),
+            pltpu.VMEM((ngroup, blk, LANES), BF16),
+            pltpu.VMEM((nhead, mem * blk, LANES), BF16),
+            pltpu.VMEM((nhead, mem * blk, LANES), BF16),
+            pltpu.VMEM((nfar, 7, mem * blk, LANES), BF16),
+            pltpu.VMEM((nfar, mem * blk, LANES), BF16),
+            pltpu.VMEM((nfar, mem * blk, LANES), BF16),
+            pltpu.VMEM((width // DK, mem * seq, qrows), F32),
+            pltpu.VMEM((ngroup * mem, blk, LANES), F32),
+            pltpu.VMEM((ngroup, blk, LANES), BF16),
+            pltpu.VMEM((ngroup - 1, blk, LANES), BF16),
+            pltpu.VMEM((nhead, blk, LANES), BF16),
+            dma((12,)),
+            dma,
+            dma((nchip,)),
+            dma,
+            dma,
+            dma,
+            dma((2, nchip)),
+            dma,
+            dma((2,)),
+            dma((nfar,)),
+            dma((nfar,)),
+            dma((8,)),
+            dma((6,)),
+            pltpu.SemaphoreType.REGULAR,
+        ],
+        compiler_params=pltpu.CompilerParams(
+            collective_id=0, has_side_effects=True, vmem_limit_bytes=40 * 1024 * 1024
+        ),
+    )(
+        *(pltpu.with_memory_space_constraint(x, pltpu.HBM) for x in operands),
+    )
     return tuple(
         pl.pallas_call(
-            functools.partial(kernel, ngroup, nhead, mem),
-            out_shape=(
-                pltpu.VMEM((qrows, width), BF16),
-                pltpu.VMEM((seq, dim), BF16),
-            ),
-            in_specs=[hbm] * 12,
-            out_specs=(vmem, vmem),
-            scratch_shapes=[
-                pltpu.SMEM(sources.shape[::-1], jnp.int32),
-                pltpu.SMEM(head_keep.shape, jnp.int32),
-                pltpu.VMEM(enc_resid.shape, BF16),
-                pltpu.VMEM(enc_qkv.shape, BF16),
-                pltpu.VMEM(enc_bias.shape, F32),
-                pltpu.VMEM((chunks, LANES), F32),
-                pltpu.VMEM(cross_bias.shape[::-1], F32),
-                pltpu.VMEM((ngroup,) + out_weight.shape, BF16),
-                pltpu.VMEM((ngroup,) + key_weight.shape, BF16),
-                pltpu.VMEM((ngroup,) + value_weight.shape, BF16),
-                pltpu.VMEM((qrows, width), BF16),
-                pltpu.VMEM((qrows, width), BF16),
-                pltpu.VMEM((mem * seq * chunks, LANES), F32),
-                pltpu.VMEM((seq * chunks, LANES), F32),
-                pltpu.VMEM((nhead, blk, LANES), BF16),
-                pltpu.VMEM((nhead - 1, blk, LANES), BF16),
-                pltpu.VMEM((ngroup, blk, LANES), BF16),
-                pltpu.VMEM((nhead, mem * blk, LANES), BF16),
-                pltpu.VMEM((nhead, mem * blk, LANES), BF16),
-                pltpu.VMEM((nfar, 7, mem * blk, LANES), BF16),
-                pltpu.VMEM((nfar, mem * blk, LANES), BF16),
-                pltpu.VMEM((nfar, mem * blk, LANES), BF16),
-                pltpu.VMEM((ngroup, mem * blk, LANES), BF16),
-                pltpu.VMEM((nhead, blk, LANES), BF16),
-                dma((12,)),
-                dma,
-                dma((nchip,)),
-                dma,
-                dma,
-                dma,
-                dma((2, nchip)),
-                dma,
-                dma,
-                dma((nfar,)),
-                dma((nfar,)),
-                dma((8,)),
-                dma((6,)),
-                pltpu.SemaphoreType.REGULAR,
-            ],
-            compiler_params=pltpu.CompilerParams(
-                collective_id=0, has_side_effects=True, vmem_limit_bytes=40 * 1024 * 1024
-            ),
-        )(
-            *(pltpu.with_memory_space_constraint(x, pltpu.HBM) for x in operands),
-        )
+            store,
+            out_shape=tuple(pltpu.HBM(x.shape, x.dtype) for x in held),
+            in_specs=[vmem, vmem],
+            out_specs=(hbm, hbm),
+            scratch_shapes=[dma((2,))],
+        )(*(pltpu.with_memory_space_constraint(x, pltpu.VMEM) for x in held))
     )
 
 

time: 87.3 us -> 83.5 us (0.956)
  Pallas kernels: 85.2 us -> 82.7 us
  local copies, waits for them, and re-layouts: 1.4 us -> 0 us
    pallas_call x1, Pallas kernels: 85.2 us -> 81.9 us  [shards(): pl.pallas_call(functools.partial(kernel, ngroup, nhead, mem), out_shape=(...]
    unnamed x2 -> x0, local copies, waits for them, and re-layouts: 1.4 us -> none
where the time goes in v4:
time: 83.5 us; the launch traced here: 83.4 us
  Pallas kernels  82.7 us (99%)
    pallas_call x1, Pallas kernels, shards(): pl.pallas_call(functools.partial(kernel, ngroup, nhead, mem), out_shape=(...  81.9 us

profile of v4, /device:TPU:1, one launch (start us, length us, event | category | flops | bytes accessed | tf_op | source)
XLA Modules:
  0.0 83.4 jit_solution(9819493445451400073)
XLA Ops:
  0.6 81.9 %shard_map.131 = (bf16[384,512]{1,0:T(8,128)(2,1)S(1)}, bf16[64,1024]{1,0:T(8,128)(2,1)S(1)}) custom-call(s32[3,16]{1,0:T(4,128)} %bitcast.5, s32[1,4]{1,0:T(1,128)} %keep_hbm.1, bf16[64,1024]{1,0:T(8,128)(2,1)} %resid_hbm.1, bf16[3,64,512]{2,1,0:T(8,128)(2,1)} %qkv_hbm.1, f32[64,64]{1,0:T(8,128)} %enc_bias_hbm.1, f32[8,128]{1,0:T(8,128)} %bitcast.4, ...), custom_call_target="tpu_custom_call" | custom-call | tf_op jit(solution)/shard_map/pallas_call | solution.py:440
  82.6 0.8 shard_map.132

commit v5 on v4

--- a/solution.py
+++ b/solution.py
@@ -176,10 +176,13 @@
     def _():
         pl.semaphore_wait(ready, 1)
 
+    locals_[2].wait()
     for i, (dx, dy) in enumerate(chip_steps):
-        remote(out_w, wo.at[g], wo_send, wo_recv.at[i], {"group": group_at(dx, dy, 0)}).start()
-    remote(out_w, wo.at[g], wo_pass_send, wo_pass_recv, {"group": sibling}).start()
-
+        remote(wo.at[g], wo.at[g], wo_send, wo_recv.at[i], {"group": group_at(dx, dy, 0)}).start()
+    remote(wo.at[g], wo.at[g], wo_pass_send, wo_pass_recv, {"group": sibling}).start()
+
+    locals_[3].wait()
+    locals_[4].wait()
     locals_[5].wait()
     locals_[6].wait()
     bias = enc_bias[...]
@@ -219,7 +222,6 @@
         pl.semaphore_wait(barrier, 2 * (nhead - 1))
         tell_sibling()
 
-    locals_[2].wait()
     total(wo.at[pl.ds(0, nchip)], wo_pass_send, wo_pass_recv).wait_recv()
     part = mm(ctx, wo[...].reshape(width, dim), 1, 0)
 
@@ -234,9 +236,26 @@
         there = head_at(*step)
         remote(out_send.at[there], out_recv.at[i], phase_send.at[0], phase_recv.at[0], {"head": there}).start()
 
-    for i, (dx, dy) in enumerate(chip_steps):
-        remote(key_w, kw.at[g], kv_send, kv_recv.at[0, i], {"group": group_at(dx, dy, 0)}).start()
-    remote(key_w, kw.at[g], kv_pass_send, kv_pass_recv.at[0], {"group": sibling}).start()
+    across = chip_steps.index((0, 1))
+    along = [(i, dx) for i, (dx, dy) in enumerate(chip_steps) if dy == 0]
+
+    def send_weight(j, ref):
+        there = ref.at[g]
+        remote(there, there, kv_send, kv_recv.at[j, across], {"group": group_at(0, 1, 0)}).start()
+        for i, dx in along:
+            remote(there, there, kv_send, kv_recv.at[j, i], {"group": group_at(dx, 0, 0)}).start()
+        remote(there, there, kv_pass_send, kv_pass_recv.at[j], {"group": sibling}).start()
+
+    def relay_weight(j, ref):
+        there = ref.at[group_at(0, 1, 0)]
+        remote(there, there, kv_send, kv_recv.at[j, across], {"group": sibling}).wait_recv()
+        for _, dx in along:
+            i = chip_steps.index((dx, 1))
+            remote(there, there, kv_send, kv_recv.at[j, i], {"group": group_at(dx, 0, 0)}).start()
+        remote(there, there, kv_pass_send, kv_pass_recv.at[j], {"group": sibling}).start()
+
+    send_weight(0, kw)
+    relay_weight(0, kw)
 
     mine = pl.ds(pl.multiple_of(h * blk, blk), blk)
     memory = flat[mine, :] + resid_flat[mine, :]
@@ -265,17 +284,19 @@
     there = norm_pick.at[h]
     for i, a in enumerate(far_steps):
         remote(there, there, phase_send.at[2], far_recv.at[i], {"head": head_at(a, 0)}).start()
-    for i, (dx, dy) in enumerate(chip_steps):
-        remote(value_w, vw.at[g], kv_send, kv_recv.at[1, i], {"group": group_at(dx, dy, 0)}).start()
-    remote(value_w, vw.at[g], kv_pass_send, kv_pass_recv.at[1], {"group": sibling}).start()
+    send_weight(1, vw)
 
     def pass_kv(j, ref):
         for i, (dx, dy) in enumerate(chip_steps):
+            if i == across:
+                continue
             there = ref.at[group_at(nx - dx, dy, 0)]
             remote(there, there, kv_send, kv_recv.at[j, i], {"group": sibling}).wait_recv()
             remote(there, there, kv_pass_send, kv_pass_recv.at[j], {"group": sibling}).start()
 
     pass_kv(0, kw)
+
+    relay_weight(1, vw)
 
     nfar = len(far_steps)
     npass = nfar * len(near_steps) - 1
@@ -286,7 +307,7 @@
             if (a + b) % nz or dy:
                 remote(there, there, phase_send.at[6], phase_recv.at[2], {"head": head_at(b, dy)}).start()
     pass_kv(1, vw)
-    for i in (0, 3, 9, 11):
+    for i in (0, 9, 11):
         locals_[i].wait()
     total(kw.at[pl.ds(0, nchip)], kv_pass_send, kv_pass_recv.at[0]).wait_recv()
     total(norm_pick.at[pl.ds(0, npass)], phase_send.at[6], phase_recv.at[2]).wait_recv()
@@ -308,7 +329,6 @@
         probs[n] = e * (1.0 / jnp.sum(e, axis=0, keepdims=True))
 
     locals_[1].wait()
-    locals_[4].wait()
     total(vw.at[pl.ds(0, nchip)], kv_pass_send, kv_pass_recv.at[1]).wait_recv()
     value_full = vw[...].reshape(dim, width)
     values = mm(picked, value_full, 1, 0).astype(BF16)

time: 83.5 us -> 81.6 us (0.977)
  Pallas kernels: 82.7 us -> 80.8 us
    pallas_call x1, Pallas kernels: 81.9 us -> 80 us  [shards(): pl.pallas_call(functools.partial(kernel, ngroup, nhead, mem), out_shape=(...]
where the time goes in v5:
time: 81.6 us; the launch traced here: 81.4 us
  Pallas kernels  80.8 us (99%)
    pallas_call x1, Pallas kernels, shards(): pl.pallas_call(functools.partial(kernel, ngroup, nhead, mem), out_shape=(...  80 us

profile of v5, /device:TPU:1, one launch (start us, length us, event | category | flops | bytes accessed | tf_op | source)
XLA Modules:
  0.0 81.4 jit_solution(10884513303413333311)
XLA Ops:
  0.6 80.0 %shard_map.131 = (bf16[384,512]{1,0:T(8,128)(2,1)S(1)}, bf16[64,1024]{1,0:T(8,128)(2,1)S(1)}) custom-call(s32[3,16]{1,0:T(4,128)} %bitcast.5, s32[1,4]{1,0:T(1,128)} %keep_hbm.1, bf16[64,1024]{1,0:T(8,128)(2,1)} %resid_hbm.1, bf16[3,64,512]{2,1,0:T(8,128)(2,1)} %qkv_hbm.1, f32[64,64]{1,0:T(8,128)} %enc_bias_hbm.1, f32[8,128]{1,0:T(8,128)} %bitcast.4, ...), custom_call_target="tpu_custom_call" | custom-call | tf_op jit(solution)/shard_map/pallas_call | solution.py:460
  80.6 0.8 shard_map.132

commit v6 on v5

--- a/solution.py
+++ b/solution.py
@@ -149,7 +149,8 @@
 
     each(nchip, lambda k: hello(group=lax.rem(chip + k, nchip) * 2))
     pl.when(core == 1)(lambda: hello(group=even))
-    each(nhead, lambda k: hello(group=odd, head=head_peer(k)))
+    for step in head_steps:
+        hello(group=odd, head=head_at(*step))
     locals_ = [
         pltpu.make_async_copy(query_hbm, query, local_sem.at[0]),
         pltpu.make_async_copy(grad_hbm, grad, local_sem.at[1]),
@@ -254,38 +255,6 @@
             remote(there, there, kv_send, kv_recv.at[j, i], {"group": group_at(dx, 0, 0)}).start()
         remote(there, there, kv_pass_send, kv_pass_recv.at[j], {"group": sibling}).start()
 
-    send_weight(0, kw)
-    relay_weight(0, kw)
-
-    mine = pl.ds(pl.multiple_of(h * blk, blk), blk)
-    memory = flat[mine, :] + resid_flat[mine, :]
-    total(out_recv, phase_send.at[0], phase_recv.at[0]).wait_recv()
-    memory = memory + jnp.sum(out_recv[...].astype(F32), axis=0)
-
-    def row_mean(x):
-        x3 = x.reshape(own_rows, chunks, LANES)
-        m = jnp.sum(jnp.sum(x3, axis=1, keepdims=True), axis=2, keepdims=True) * (1.0 / dim)
-        return jnp.broadcast_to(m, x3.shape).reshape(blk, LANES)
-
-    locals_[8].wait()
-    gains = jnp.broadcast_to(gain[...][None], (own_rows, chunks, LANES)).reshape(blk, LANES)
-    inv = lax.rsqrt(row_mean(memory * memory) + EPS)
-    normed = memory * inv
-    norm_all[g] = (normed * gains).astype(BF16)
-
-    there = norm_all.at[g]
-    for step in group_steps:
-        remote(there, there, phase_send.at[1], phase_recv.at[1], {"group": group_at(*step)}).start()
-    total(norm_all.at[pl.ds(0, ngroup - 1)], phase_send.at[1], phase_recv.at[1]).wait_recv()
-
-    for s in range(mem):
-        norm_pick[h, s * blk : (s + 1) * blk, :] = norm_all[sources[s, g]]
-
-    there = norm_pick.at[h]
-    for i, a in enumerate(far_steps):
-        remote(there, there, phase_send.at[2], far_recv.at[i], {"head": head_at(a, 0)}).start()
-    send_weight(1, vw)
-
     def pass_kv(j, ref):
         for i, (dx, dy) in enumerate(chip_steps):
             if i == across:
@@ -294,7 +263,38 @@
             remote(there, there, kv_send, kv_recv.at[j, i], {"group": sibling}).wait_recv()
             remote(there, there, kv_pass_send, kv_pass_recv.at[j], {"group": sibling}).start()
 
+    send_weight(0, kw)
+    relay_weight(0, kw)
+
+    mine = pl.ds(pl.multiple_of(h * blk, blk), blk)
+    memory = flat[mine, :] + resid_flat[mine, :]
+    total(out_recv, phase_send.at[0], phase_recv.at[0]).wait_recv()
+    memory = memory + jnp.sum(out_recv[...].astype(F32), axis=0)
+
+    def row_mean(x):
+        x3 = x.reshape(own_rows, chunks, LANES)
+        m = jnp.sum(jnp.sum(x3, axis=1, keepdims=True), axis=2, keepdims=True) * (1.0 / dim)
+        return jnp.broadcast_to(m, x3.shape).reshape(blk, LANES)
+
+    locals_[8].wait()
+    gains = jnp.broadcast_to(gain[...][None], (own_rows, chunks, LANES)).reshape(blk, LANES)
+    inv = lax.rsqrt(row_mean(memory * memory) + EPS)
+    normed = memory * inv
+    norm_all[g] = (normed * gains).astype(BF16)
+
+    there = norm_all.at[g]
+    for step in group_steps:
+        remote(there, there, phase_send.at[1], phase_recv.at[1], {"group": group_at(*step)}).start()
     pass_kv(0, kw)
+    total(norm_all.at[pl.ds(0, ngroup - 1)], phase_send.at[1], phase_recv.at[1]).wait_recv()
+
+    for s in range(mem):
+        norm_pick[h, s * blk : (s + 1) * blk, :] = norm_all[sources[s, g]]
+
+    there = norm_pick.at[h]
+    for i, a in enumerate(far_steps):
+        remote(there, there, phase_send.at[2], far_recv.at[i], {"head": head_at(a, 0)}).start()
+    send_weight(1, vw)
 
     relay_weight(1, vw)
 

time: 81.6 us -> 81.3 us (level)
  no operation moved by 1% of the time
where the time goes in v6:
time: 81.3 us; the launch traced here: 81.1 us
  Pallas kernels  80.5 us (99%)
    pallas_call x1, Pallas kernels, shards(): pl.pallas_call(functools.partial(kernel, ngroup, nhead, mem), out_shape=(...  79.7 us

profile of v6, /device:TPU:1, one launch (start us, length us, event | category | flops | bytes accessed | tf_op | source)
XLA Modules:
  0.0 81.1 jit_solution(6153451354634202076)
XLA Ops:
  0.6 79.7 %shard_map.131 = (bf16[384,512]{1,0:T(8,128)(2,1)S(1)}, bf16[64,1024]{1,0:T(8,128)(2,1)S(1)}) custom-call(s32[3,16]{1,0:T(4,128)} %bitcast.5, s32[1,4]{1,0:T(1,128)} %keep_hbm.1, bf16[64,1024]{1,0:T(8,128)(2,1)} %resid_hbm.1, bf16[3,64,512]{2,1,0:T(8,128)(2,1)} %qkv_hbm.1, f32[64,64]{1,0:T(8,128)} %enc_bias_hbm.1, f32[8,128]{1,0:T(8,128)} %bitcast.4, ...), custom_call_target="tpu_custom_call" | custom-call | tf_op jit(solution)/shard_map/pallas_call | solution.py:460
  80.3 0.8 shard_map.132

commit v7 on v6

--- a/solution.py
+++ b/solution.py
@@ -147,7 +147,8 @@
     def tell_sibling():
         pl.semaphore_signal(ready, inc=1, device_id={"group": sibling}, device_id_type=MESH)
 
-    each(nchip, lambda k: hello(group=lax.rem(chip + k, nchip) * 2))
+    for step in chip_steps:
+        hello(group=group_at(*step, 0) - core)
     pl.when(core == 1)(lambda: hello(group=even))
     for step in head_steps:
         hello(group=odd, head=head_at(*step))

time: 81.3 us -> 81.5 us (level)
  no operation moved by 1% of the time
where the time goes in v7:
time: 81.5 us; the launch traced here: 81.3 us
  Pallas kernels  80.7 us (99%)
    pallas_call x1, Pallas kernels, shards(): pl.pallas_call(functools.partial(kernel, ngroup, nhead, mem), out_shape=(...  79.9 us

profile of v7, /device:TPU:1, one launch (start us, length us, event | category | flops | bytes accessed | tf_op | source)
XLA Modules:
  0.0 81.3 jit_solution(14674837017221879489)
XLA Ops:
  0.6 79.9 %shard_map.131 = (bf16[384,512]{1,0:T(8,128)(2,1)S(1)}, bf16[64,1024]{1,0:T(8,128)(2,1)S(1)}) custom-call(s32[3,16]{1,0:T(4,128)} %bitcast.5, s32[1,4]{1,0:T(1,128)} %keep_hbm.1, bf16[64,1024]{1,0:T(8,128)(2,1)} %resid_hbm.1, bf16[3,64,512]{2,1,0:T(8,128)(2,1)} %qkv_hbm.1, f32[64,64]{1,0:T(8,128)} %enc_bias_hbm.1, f32[8,128]{1,0:T(8,128)} %bitcast.4, ...), custom_call_target="tpu_custom_call" | custom-call | tf_op jit(solution)/shard_map/pallas_call | solution.py:461
  80.5 0.8 shard_map.132
